TPU v7x, 32 devices: a whole 2x2x4 slice. The times are simulated.
32 devices in a mesh: groups: 2 (over y), pairs: 8 (over z, x), rows: 2 (over core).
Axes of the slice: x: 2, y: 2, z: 4, core: 2. Of those that a mesh axis runs over, the one named last changes fastest.
Arguments:
- first_image: float32 [16, 128, 256], P(('groups', 'pairs'), 'rows'), parts along dimension 0, may hold values from -12 to 12
- second_image: float32 [16, 128, 256], P(('groups', 'pairs'), 'rows'), parts along dimension 0, may hold values from -12 to 12
- prior_motion: float32 [2, 16, 128, 256], P(None, ('groups', 'pairs'), 'rows'), parts along dimension 1, may hold values from -40 to 40
- offsets: int32 [64, 2], replicated, may hold values from -4 to 4, as said below
- pair_epochs: int32 [16, 2], P('groups'), parts along dimension 0, may hold values from 0 to 128, as said below
- pair_slot: int32 [16], P('groups'), parts along dimension 0, may hold values from 0 to 7, each once
Outputs:
- velocity: float32 [2, 128, 4, 16384], P(None, None, ('groups', 'rows'), 'pairs'), parts along dimension 2
- motion: float32 [2, 16, 128, 256], P(None, ('groups', 'pairs'), 'rows'), parts along dimension 1
There are 2 independent parts, one for each index of `groups`. A program takes and returns all parts, laid end to end along the dimension named above; an argument that names none is the same for every part. Nothing has to cross between parts.
Inputs may be any that keep to these rules, and one draw needn't show every extreme that they name: 64 distinct offsets; every offset with a component of magnitude 4 is among them. `pair_epochs`: each row has first < after. `pair_slot`: a permutation of the pairs.
All inputs are finite; a program needn't handle non-finite values. Where the computation divides by a largest or mean magnitude, that divisor is 1e-20 or more.
Results may differ from a plain program's by a relative error of at most 0.0003.
Values sent between devices are 32-bit elements; how exact they have to be, the bound alone decides.
A program may use at most 64 MiB of HBM per device.

v0:
```python
import functools

import jax
import jax.numpy as jnp
from jax import lax
from jax.experimental import pallas as pl
from jax.experimental.pallas import tpu as pltpu
from jax.sharding import PartitionSpec as P

SEARCH = 4
RADIUS = 4
EPOCHS = 128
ITERS = 4
ROUNDS = 2

SOFTMIN_HEAT = 0.1
PRIOR_STRENGTH = 0.05
PENALTY = 4.0
SPARSITY = 0.4
VARIANCE_FLOOR = 0.05
HIGHEST = lax.Precision.HIGHEST

SIDE = 2 * SEARCH + 1
WINDOW = 2 * RADIUS + 1
MARGIN = SEARCH + RADIUS
SUB = 8
LANES = 128
AREA = 1.0 / float(WINDOW * WINDOW)
VMEM_BYTES = 40 * 1024 * 1024
BLOCK = 4


def vmem_spec():
    return pl.BlockSpec(memory_space=pltpu.VMEM)


def smem_spec():
    return pl.BlockSpec(memory_space=pltpu.SMEM)


def params(**more):
    return pltpu.CompilerParams(vmem_limit_bytes=VMEM_BYTES, **more)


def parts_of(values):
    high = values.astype(jnp.bfloat16)
    rest = values - high.astype(jnp.float32)
    middle = rest.astype(jnp.bfloat16)
    low = (rest - middle.astype(jnp.float32)).astype(jnp.bfloat16)
    return high, middle, low


def band_matrix(columns, shift):
    row = lax.broadcasted_iota(jnp.int32, (columns, columns), 0)
    col = lax.broadcasted_iota(jnp.int32, (columns, columns), 1)
    return (jnp.abs(row - col - shift) <= RADIUS).astype(jnp.float32).astype(jnp.bfloat16)


def column_box(values, band):
    high, middle, low = parts_of(values)
    mm = functools.partial(jnp.dot, preferred_element_type=jnp.float32)
    return mm(high, band) + (mm(middle, band) + mm(low, band))


def row_box(planes, count):
    result = []
    for base in range(0, count, SUB):
        mid = base + WINDOW - 2
        suffix = {mid: planes[mid]}
        for i in range(mid - 1, base - 1, -1):
            suffix[i] = planes[i] + suffix[i + 1]
        prefix = {mid + 1: planes[mid + 1]}
        for i in range(mid + 2, base + SUB - 1 + WINDOW):
            prefix[i] = prefix[i - 1] + planes[i]
        for i in range(base, base + SUB):
            result.append(suffix[i] + prefix[i + WINDOW - 1])
    return result


def inverse_root(values):
    guess = lax.rsqrt(values)
    return guess * (1.5 - 0.5 * values * guess * guess)


def split_lanes(values):
    return jnp.stack([values[:, i : i + LANES] for i in range(0, values.shape[1], LANES)])


def strided(ref, start, stride):
    rows = pl.ds(start, SUB, stride=stride)
    return jnp.concatenate([ref[i, rows, :] for i in range(ref.shape[0])], axis=-1)


def store_strided(ref, start, stride, values):
    rows = pl.ds(start, SUB, stride=stride)
    for i in range(ref.shape[0]):
        ref[i, rows, :] = values[:, i * LANES : (i + 1) * LANES]


def prepare(image_ref, f_ref, s_ref, mean_ref, inv_ref, mean1_ref, inv1_ref):
    rows = image_ref.shape[2] - 2 * MARGIN
    columns = image_ref.shape[1] * LANES
    steps = rows // SUB
    band = band_matrix(columns, 0)

    raw = [strided(image_ref.at[0], SEARCH + t, steps) for t in range(steps + 2 * RADIUS)]
    scaled = [x * AREA for x in raw]
    for t, x in enumerate(scaled):
        f_ref[t] = x
    sums = row_box(scaled, steps) + row_box([a * b for a, b in zip(raw, scaled)], steps)
    boxed = column_box(jnp.concatenate(sums, axis=0), band)
    mean1 = boxed[:rows]
    var1 = boxed[rows:] - mean1 * mean1
    mean1_ref[...] = mean1.reshape(steps, SUB, columns)
    inv1 = inverse_root(jnp.maximum(var1, VARIANCE_FLOOR)) * (1.0 / SOFTMIN_HEAT)
    inv1_ref[...] = inv1.reshape(steps, SUB, columns)

    reach = steps + 2 * MARGIN
    second = [strided(image_ref.at[1], t, steps) for t in range(reach)]
    wide = steps + 2 * SEARCH
    sums = row_box(second, wide) + row_box([x * x for x in second], wide)
    sums = parts_of(jnp.concatenate(sums, axis=0))
    stacked = jnp.concatenate(second, axis=0)
    lane = lax.broadcasted_iota(jnp.int32, stacked.shape, 1)
    half = wide * SUB
    for place in range(SIDE):
        shift = place - SEARCH
        moved = pltpu.roll(stacked, (-shift) % columns, 1) if shift else stacked
        inside = (lane + shift >= 0) & (lane + shift < columns)
        s_ref[place] = jnp.where(inside, moved, 0.0).reshape(reach, SUB, columns)
        shifted_band = band_matrix(columns, shift)
        mm = functools.partial(jnp.dot, preferred_element_type=jnp.float32)
        boxed = mm(sums[0], shifted_band) + (
            mm(sums[1], shifted_band) + mm(sums[2], shifted_band)
        )
        boxed = boxed * AREA
        mean = boxed[:half]
        var = boxed[half:] - mean * mean
        mean_ref[place] = mean.reshape(wide, SUB, columns)
        inv = inverse_root(jnp.maximum(var, VARIANCE_FLOOR))
        inv_ref[place] = inv.reshape(wide, SUB, columns)


def correlate(offsets_ref, f_ref, s_ref, mean_ref, inv_ref, mean1_ref, inv1_ref, e_ref):
    steps, _, columns = mean1_ref.shape
    rows = steps * SUB
    band = band_matrix(columns, 0)
    count = offsets_ref.shape[0]
    block = BLOCK if count % BLOCK == 0 else 1

    def body(number, carry):
        sums = []
        for i in range(block):
            k = number * block + i
            oy = offsets_ref[k, 0] + SEARCH
            ox = offsets_ref[k, 1] + SEARCH
            planes = [f_ref[t] * s_ref[ox, oy + t] for t in range(steps + 2 * RADIUS)]
            sums += row_box(planes, steps)
        boxed = column_box(jnp.concatenate(sums, axis=0), band)
        for i in range(block):
            k = number * block + i
            oy = offsets_ref[k, 0] + SEARCH
            ox = offsets_ref[k, 1] + SEARCH
            for t in range(steps):
                at = i * rows + t * SUB
                cov = boxed[at : at + SUB] - mean1_ref[t] * mean_ref[ox, oy + t]
                e_ref[k, t] = jnp.exp(cov * (inv1_ref[t] * inv_ref[ox, oy + t]))
        return carry

    lax.fori_loop(0, count // block, body, 0)


def prior_tables(prior_row, prior_col, a_ref, b_ref, lanes):
    steps = a_ref.shape[1]
    curve = 0.5 * (2.0 * PRIOR_STRENGTH / SOFTMIN_HEAT)
    for t in range(steps):
        for ref, prior in ((a_ref, prior_row(t)), (b_ref, prior_col(t))):
            near = jnp.clip(jnp.floor(prior + 0.5), -float(SEARCH), float(SEARCH))
            twice = near - 2.0 * prior
            for place in range(SIDE):
                i = float(place - SEARCH)
                ref[place, t, :, lanes] = jnp.exp(curve * ((near - i) * (twice + i)))


def match(offsets_ref, e_ref, a_ref, b_ref, lanes, together, store):
    count, steps = e_ref.shape[:2]
    for base in range(0, steps, together):
        here = pl.ds(base, together)
        zero = jnp.zeros((together, SUB, lanes.size), jnp.float32)

        def body(k, carry):
            total, rows, cols = carry
            oy = offsets_ref[k, 0]
            ox = offsets_ref[k, 1]
            table = a_ref[oy + SEARCH, here, :, lanes] * b_ref[ox + SEARCH, here, :, lanes]
            weight = e_ref[k, here, :, lanes] * table
            return (
                total + weight,
                rows + weight * oy.astype(jnp.float32),
                cols + weight * ox.astype(jnp.float32),
            )

        total, rows, cols = lax.fori_loop(0, count, body, (zero, zero, zero), unroll=8)
        for i in range(together):
            store(base + i, rows[i] / total[i], cols[i] / total[i])


def design_kernel(epochs_ref, slot_ref, coef_ref, seg_ref, ends_ref):
    pairs = slot_ref.shape[0]
    ends = 2 * pairs
    row_id = lax.broadcasted_iota(jnp.int32, (pairs, pairs), 0)
    col_id = lax.broadcasted_iota(jnp.int32, (pairs, pairs), 1)
    end_id = lax.broadcasted_iota(jnp.int32, (ends, pairs), 0)
    end_col = lax.broadcasted_iota(jnp.int32, (ends, pairs), 1)
    seg_id = lax.broadcasted_iota(jnp.int32, (ends, EPOCHS), 0)
    epoch = lax.broadcasted_iota(jnp.int32, (ends, EPOCHS), 1)

    def gather(j, state):
        first_r, after_r, first_c, after_c, mark, mark_e, first_e, after_e = state
        first = epochs_ref[slot_ref[j], 0]
        after = epochs_ref[slot_ref[j], 1]
        ends_ref[0, j] = first
        ends_ref[1, j] = after
        return (
            jnp.where(row_id == j, first, first_r),
            jnp.where(row_id == j, after, after_r),
            jnp.where(col_id == j, first, first_c),
            jnp.where(col_id == j, after, after_c),
            jnp.where(end_id == j, first, jnp.where(end_id == j + pairs, after, mark)),
            jnp.where(seg_id == j, first, jnp.where(seg_id == j + pairs, after, mark_e)),
            jnp.where(end_col == j, first, first_e),
            jnp.where(end_col == j, after, after_e),
        )

    square = jnp.zeros((pairs, pairs), jnp.int32)
    tall = jnp.zeros((ends, pairs), jnp.int32)
    state = (square, square, square, square, tall, jnp.zeros((ends, EPOCHS), jnp.int32), tall, tall)
    first_r, after_r, first_c, after_c, mark, mark_e, first_e, after_e = lax.fori_loop(
        0, pairs, gather, state
    )
    overlap = jnp.maximum(jnp.minimum(after_r, after_c) - jnp.maximum(first_r, first_c), 0)
    matrix = overlap.astype(jnp.float32) + jnp.where(row_id == col_id, PENALTY, 0.0)

    def eliminate(j, a):
        on_row = row_id == j
        on_col = col_id == j
        row = jnp.sum(jnp.where(on_row, a, 0.0), axis=0, keepdims=True)
        col = jnp.sum(jnp.where(on_col, a, 0.0), axis=1, keepdims=True)
        pivot = jnp.sum(jnp.where(col_id[:1] == j, row, 0.0), axis=1, keepdims=True)
        scale = 1.0 / pivot
        inner = a - col * (row * scale)
        return jnp.where(
            on_row,
            jnp.where(on_col, scale, row * scale),
            jnp.where(on_col, -col * scale, inner),
        )

    inverse = lax.fori_loop(0, pairs, eliminate, matrix)
    inside = ((mark >= first_e) & (mark < after_e)).astype(jnp.float32)
    coef = jnp.dot(inside, inverse, precision=HIGHEST, preferred_element_type=jnp.float32)
    wider = coef_ref.shape[1] - pairs
    if wider:
        coef = jnp.concatenate([coef, jnp.zeros((ends, wider), jnp.float32)], axis=1)
    coef_ref[...] = coef
    latest = jnp.max(jnp.where(mark_e <= epoch, mark_e, -1), axis=0, keepdims=True)
    which = jnp.max(jnp.where(mark_e == latest, seg_id, -1), axis=0, keepdims=True)
    seg_ref[...] = jnp.broadcast_to(jnp.where(latest < 0, ends, which), seg_ref.shape)


def design(pair_epochs, pair_slot):
    pairs = pair_slot.shape[0]
    return pl.pallas_call(
        design_kernel,
        out_shape=(
            jax.ShapeDtypeStruct((2 * pairs, pairs), jnp.float32),
            jax.ShapeDtypeStruct((1, EPOCHS), jnp.int32),
            jax.ShapeDtypeStruct((2, pairs), jnp.int32),
        ),
        in_specs=[smem_spec(), smem_spec()],
        out_specs=(vmem_spec(), vmem_spec(), smem_spec()),
        compiler_params=params(),
        name="design",
    )(pair_epochs, pair_slot)


def invert(coef_ref, seg_ref, ends_ref, pairs, d, begin, z, g, t_ref, cum_ref, predict):
    ends = 2 * pairs
    threshold = SPARSITY / PENALTY
    zero = jnp.zeros(t_ref.shape[1:], jnp.float32)
    t_ref[ends] = zero
    cum_ref[0] = zero
    if predict is not None:
        predict[1][0] = zero
    short = pairs <= 16

    for iteration in range(ITERS):
        start = begin is None and iteration == 0
        z_from, g_from = begin if begin and iteration == 0 else (z[0], g[0])
        last = iteration + 1 == ITERS
        summing = last and predict is not None

        def residual(p):
            return d(p) if start else d(p) - g_from(p)

        if short:
            gaps = [residual(p) for p in range(pairs)]
            for j in range(ends):
                value = coef_ref[j, 0] * gaps[0]
                for p in range(1, pairs):
                    value = value + coef_ref[j, p] * gaps[p]
                t_ref[j] = value
        else:

            def fill(j):
                t_ref[j] = lax.fori_loop(
                    0, pairs, lambda p, v: v + coef_ref[j, p] * residual(p), zero
                )

            pl.loop(0, ends)(fill)

        def epoch_step(e, carry):
            s = t_ref[seg_ref[0, e]]
            if not start:
                s = s + z_from(e)
            u = jnp.clip(s, -threshold, threshold)
            new = s - u
            z[1](e, new, last)
            if last and not summing:
                return carry
            run = carry[0] + (new - u)
            cum_ref[e + 1] = run
            if not summing:
                return (run,)
            run_z = carry[1] + new
            predict[1][e + 1] = run_z
            return (run, run_z)

        lax.fori_loop(0, EPOCHS, epoch_step, (zero, zero) if summing else (zero,), unroll=8)
        if last and not summing:
            return

        def collect(p):
            first, after = ends_ref[0, p], ends_ref[1, p]
            g[1](p, cum_ref[after] - cum_ref[first])
            if summing:
                predict[0](p, predict[1][after] - predict[1][first])

        if short:
            for p in range(pairs):
                collect(p)
        else:
            pl.loop(0, pairs)(collect)


def second_axis(ref):
    def store(i, value, last=False):
        ref[:, i] = value

    return (lambda i: ref[:, i]), store


def match_scratch(steps, columns):
    plane = (SUB, columns)
    extended = (2, columns // LANES, steps * SUB + 2 * MARGIN, LANES)
    return [
        pltpu.VMEM(extended, jnp.float32),
        pltpu.VMEM((steps + 2 * RADIUS,) + plane, jnp.float32),
        pltpu.VMEM((SIDE, steps + 2 * MARGIN) + plane, jnp.float32),
        pltpu.VMEM((SIDE, steps + 2 * SEARCH) + plane, jnp.float32),
        pltpu.VMEM((SIDE, steps + 2 * SEARCH) + plane, jnp.float32),
        pltpu.VMEM((steps,) + plane, jnp.float32),
        pltpu.VMEM((steps,) + plane, jnp.float32),
    ]


def weight_scratch(steps, columns):
    tables = [pltpu.VMEM((SIDE, steps, SUB, columns), jnp.float32)] * 2
    return tables + [pltpu.VMEM((2, columns // LANES, steps * SUB, LANES), jnp.float32)]


def match_on(offsets_ref, e_ref, prior_ref, back_ref, a_ref, b_ref, field_ref, motion_ref):
    steps = e_ref.shape[1]
    for component in range(2):
        values = prior_ref[component]
        if back_ref is not None:
            values = 0.5 * (values + back_ref[component])
        field_ref[component] = split_lanes(values)

    def prior(component):
        return lambda t: strided(field_ref.at[component], t, steps)

    def store(t, row, col):
        store_strided(field_ref.at[0], t, steps, row)
        store_strided(field_ref.at[1], t, steps, col)

    lanes = pl.ds(0, e_ref.shape[3])
    prior_tables(prior(0), prior(1), a_ref, b_ref, lanes)
    match(offsets_ref, e_ref, a_ref, b_ref, lanes, 2, store)
    for component in range(2):
        halves = [field_ref[component, i] for i in range(field_ref.shape[1])]
        motion_ref[component] = jnp.concatenate(halves, axis=-1)


def first_kernel(offsets_ref, images_ref, prior_ref, e_ref, motion_ref, *scratch):
    image_ref, *tables = scratch[:7]
    for i in range(2):
        image_ref[i] = split_lanes(images_ref[i])
    prepare(image_ref, *tables)
    correlate(offsets_ref, *tables, e_ref)
    match_on(offsets_ref, e_ref, prior_ref, None, *scratch[7:], motion_ref)


def again_kernel(offsets_ref, e_ref, prior_ref, back_ref, motion_ref, *scratch):
    match_on(offsets_ref, e_ref, prior_ref, back_ref, *scratch, motion_ref)


def invert_first_kernel(coef_ref, seg_ref, ends_ref, d_ref, z_ref, g_ref, gz_ref, t_ref, cum_ref, cumz_ref):
    z, g, d, gz = (second_axis(ref) for ref in (z_ref, g_ref, d_ref, gz_ref))
    tables = (coef_ref, seg_ref, ends_ref, d_ref.shape[1])
    invert(*tables, d[0], None, z, g, t_ref, cum_ref, (gz[1], cumz_ref))


def invert_last_kernel(coef_ref, seg_ref, ends_ref, d_ref, zin_ref, gin_ref, z_ref, g_ref, t_ref, cum_ref):
    z, g, d = (second_axis(ref) for ref in (z_ref, g_ref, d_ref))
    begin = (second_axis(zin_ref)[0], second_axis(gin_ref)[0])
    tables = (coef_ref, seg_ref, ends_ref, d_ref.shape[1])
    invert(*tables, d[0], begin, z, g, t_ref, cum_ref, None)


def fused_kernel(
    offsets_ref,
    epochs_ref,
    slot_ref,
    first_ref,
    second_ref,
    prior_ref,
    velocity_ref,
    motion_ref,
    image_ref,
    f_ref,
    s_ref,
    mean_ref,
    inv_ref,
    mean1_ref,
    inv1_ref,
    a_ref,
    b_ref,
    field_ref,
    e_ref,
    prior_split_ref,
    back_ref,
    edge_ref,
    halo_ref,
    d_ref,
    gz_ref,
    z_ref,
    g_ref,
    t_ref,
    cum_ref,
    cumz_ref,
    coef_vmem,
    seg_vmem,
    coef_ref,
    seg_ref,
    ends_ref,
    table_sem,
    halo_sem,
    send_sem,
    recv_sem,
):
    rows, columns = first_ref.shape
    steps = rows // SUB
    halves = columns // LANES
    pairs = slot_ref.shape[0]
    part = rows // pairs
    me = lax.axis_index("pairs")
    band = lax.axis_index("rows")
    mesh_id = pl.DeviceIdType.MESH

    barrier = pltpu.get_barrier_semaphore()
    peers = [lax.rem(me + i, pairs) for i in range(1, pairs)]
    pl.semaphore_signal(barrier, inc=1, device_id={"rows": 1 - band}, device_id_type=mesh_id)
    for peer in peers:
        pl.semaphore_signal(barrier, inc=1, device_id={"pairs": peer}, device_id_type=mesh_id)
    edge = pl.ds(pl.multiple_of((1 - band) * (rows - MARGIN), SUB), MARGIN)
    edge_ref[0] = first_ref[edge, :]
    edge_ref[1] = second_ref[edge, :]
    pl.semaphore_wait(barrier, pairs)
    halo = pltpu.make_async_remote_copy(
        src_ref=edge_ref,
        dst_ref=halo_ref,
        send_sem=halo_sem.at[0],
        recv_sem=halo_sem.at[1],
        device_id={"rows": 1 - band},
        device_id_type=mesh_id,
    )
    halo.start()

    design_kernel(epochs_ref, slot_ref, coef_vmem, seg_vmem, ends_ref)
    moves = [
        pltpu.make_async_copy(coef_vmem, coef_ref, table_sem.at[0]),
        pltpu.make_async_copy(seg_vmem, seg_ref, table_sem.at[1]),
    ]
    for move in moves:
        move.start()
    everywhere = pl.ds(0, columns)
    for component in range(2):
        prior_split_ref[component] = split_lanes(prior_ref[component])
    prior_tables(
        lambda t: strided(prior_split_ref.at[0], t, steps),
        lambda t: strided(prior_split_ref.at[1], t, steps),
        a_ref,
        b_ref,
        everywhere,
    )
    for i, ref in enumerate((first_ref, second_ref)):
        image_ref[i, :, MARGIN : MARGIN + rows, :] = split_lanes(ref[...])
    halo.wait()
    for i in range(2):
        arrived = split_lanes(halo_ref[i])
        image_ref[i, :, :MARGIN, :] = jnp.where(band == 1, arrived, 0.0)
        image_ref[i, :, MARGIN + rows :, :] = jnp.where(band == 0, arrived, 0.0)
    for move in moves:
        move.wait()
    prepare(image_ref, f_ref, s_ref, mean_ref, inv_ref, mean1_ref, inv1_ref)
    correlate(offsets_ref, f_ref, s_ref, mean_ref, inv_ref, mean1_ref, inv1_ref, e_ref)

    def block(index):
        return pl.ds(pl.multiple_of(index * part, SUB), part)

    def push(phase, half, source, target):
        copies = []
        for i, peer in enumerate(peers):
            copy = pltpu.make_async_remote_copy(
                src_ref=source(peer),
                dst_ref=target(me),
                send_sem=send_sem.at[phase, half, i],
                recv_sem=recv_sem.at[phase, half, i],
                device_id={"pairs": peer},
                device_id_type=mesh_id,
            )
            copy.start()
            copies.append(copy)
        target(me)[...] = source(me)[...]
        return copies

    def finish(copies):
        for copy in copies:
            copy.wait()

    def match_half(phase, half):
        lanes = pl.ds(half * LANES, LANES)

        def store(t, row, col):
            field_ref[0, half, pl.ds(t, SUB, stride=steps), :] = row
            field_ref[1, half, pl.ds(t, SUB, stride=steps), :] = col

        match(offsets_ref, e_ref, a_ref, b_ref, lanes, 4 if steps % 4 == 0 else 1, store)
        return push(
            phase,
            half,
            lambda q: field_ref.at[:, half, block(q), :],
            lambda q: d_ref.at[phase // 2, half, q],
        )

    def invert_half(phase, half):
        def store_z(e, value, last):
            if phase and last:
                for component in range(2):
                    place = pl.ds(half, part, stride=halves)
                    velocity_ref[component, e, place, :] = value[component]
            else:
                z_ref[half, e] = value

        def store_g(p, value):
            g_ref[half, p] = value

        def store_gz(p, value):
            gz_ref[half, p] = value

        z = ((lambda e: z_ref[half, e]), store_z)
        g = ((lambda p: g_ref[half, p]), store_g)
        invert(
            coef_ref,
            seg_ref,
            ends_ref,
            pairs,
            lambda p: d_ref[phase // 2, half, p],
            (z[0], g[0]) if phase else None,
            z,
            g,
            t_ref,
            cum_ref,
            None if phase else (store_gz, cumz_ref),
        )

    sent = [match_half(0, half) for half in range(halves)]
    returned = []
    for half in range(halves):
        finish(sent[half])
        invert_half(0, half)
        returned.append(
            push(
                1,
                half,
                lambda q: gz_ref.at[half, q],
                lambda q: back_ref.at[:, half, block(q), :],
            )
        )
    sent = []
    for half in range(halves):
        finish(returned[half])

        def prior(component):
            def at(t):
                place = pl.ds(t, SUB, stride=steps)
                given = prior_split_ref[component, half, place, :]
                return 0.5 * (given + back_ref[component, half, place, :])

            return at

        prior_tables(prior(0), prior(1), a_ref, b_ref, pl.ds(half * LANES, LANES))
        sent.append(match_half(2, half))
    for component in range(2):
        pieces = [field_ref[component, half] for half in range(halves)]
        motion_ref[component] = jnp.concatenate(pieces, axis=-1)
    for half in range(halves):
        finish(sent[half])
        invert_half(2, half)


def fused(first_image, second_image, prior, offsets, pair_epochs, pair_slot):
    rows, columns = first_image.shape
    steps, halves = rows // SUB, columns // LANES
    pairs = pair_slot.shape[0]
    part = rows // pairs
    f32 = jnp.float32
    plane = (2, part, LANES)
    split = (2, halves, rows, LANES)
    return pl.pallas_call(
        fused_kernel,
        out_shape=(
            jax.ShapeDtypeStruct((2, EPOCHS, part * halves, LANES), f32),
            jax.ShapeDtypeStruct((2, rows, columns), f32),
        ),
        in_specs=[smem_spec()] * 3 + [vmem_spec()] * 3,
        out_specs=(vmem_spec(), vmem_spec()),
        scratch_shapes=match_scratch(steps, columns)
        + weight_scratch(steps, columns)
        + [
            pltpu.VMEM((offsets.shape[0], steps, SUB, columns), f32),
            pltpu.VMEM(split, f32),
            pltpu.VMEM(split, f32),
            pltpu.VMEM((2, MARGIN, columns), f32),
            pltpu.VMEM((2, MARGIN, columns), f32),
            pltpu.VMEM((ROUNDS, halves, pairs) + plane, f32),
            pltpu.VMEM((halves, pairs) + plane, f32),
            pltpu.VMEM((halves, EPOCHS) + plane, f32),
            pltpu.VMEM((halves, pairs) + plane, f32),
            pltpu.VMEM((2 * pairs + 1,) + plane, f32),
            pltpu.VMEM((EPOCHS + 1,) + plane, f32),
            pltpu.VMEM((EPOCHS + 1,) + plane, f32),
            pltpu.VMEM((2 * pairs, LANES), f32),
            pltpu.VMEM((SUB, EPOCHS), jnp.int32),
            pltpu.SMEM((2 * pairs, LANES), f32),
            pltpu.SMEM((SUB, EPOCHS), jnp.int32),
            pltpu.SMEM((2, pairs), jnp.int32),
            pltpu.SemaphoreType.DMA((2,)),
            pltpu.SemaphoreType.DMA((2,)),
            pltpu.SemaphoreType.DMA((3, halves, pairs)),
            pltpu.SemaphoreType.DMA((3, halves, pairs)),
        ],
        compiler_params=params(collective_id=0, has_side_effects=True),
        name="track",
    )(offsets, pair_epochs, pair_slot, first_image, second_image, prior)


def with_halo(cells, axis, dim, width):
    count = lax.axis_size(axis)
    head = lax.slice_in_dim(cells, 0, width, axis=dim)
    tail = lax.slice_in_dim(cells, cells.shape[dim] - width, cells.shape[dim], axis=dim)
    down = lax.ppermute(tail, axis, [(i, i + 1) for i in range(count - 1)])
    up = lax.ppermute(head, axis, [(i + 1, i) for i in range(count - 1)])
    return jnp.concatenate([down, cells, up], axis=dim)


def per_device(first_image, second_image, prior_motion, offsets, pair_epochs, pair_slot):
    rows, columns = first_image.shape[1:]
    steps = rows // SUB
    pairs = lax.axis_size("pairs")
    pixels = rows * columns // pairs
    fold = (pixels // LANES, LANES) if pixels % LANES == 0 else (1, pixels)
    f32 = functools.partial(jax.ShapeDtypeStruct, dtype=jnp.float32)
    prior = prior_motion[:, 0]
    whole_tiles = rows % (SUB * pairs) == 0 and columns % LANES == 0 and pairs <= LANES
    if whole_tiles and lax.axis_size("rows") == 2:
        velocity, motion = fused(
            first_image[0], second_image[0], prior, offsets, pair_epochs, pair_slot
        )
        return (velocity.reshape(2, EPOCHS, 1, pixels), motion[:, None])
    coef, seg, ends = design(pair_epochs, pair_slot)
    images = with_halo(jnp.concatenate((first_image, second_image), axis=0), "rows", 1, MARGIN)
    e, motion = pl.pallas_call(
        first_kernel,
        out_shape=(f32((offsets.shape[0], steps, SUB, columns)), f32((2, rows, columns))),
        in_specs=[smem_spec(), vmem_spec(), vmem_spec()],
        out_specs=(vmem_spec(), vmem_spec()),
        scratch_shapes=match_scratch(steps, columns) + weight_scratch(steps, columns),
        compiler_params=params(),
        name="correlate",
    )(offsets, images, prior)

    def spread(field):
        outgoing = field.reshape(2, 1, pairs, pixels)
        arrived = lax.all_to_all(outgoing, "pairs", split_axis=2, concat_axis=1, tiled=True)
        return arrived.reshape((2, pairs) + fold)

    def collect(field):
        outgoing = field.reshape(2, pairs, 1, pixels)
        arrived = lax.all_to_all(outgoing, "pairs", split_axis=1, concat_axis=2, tiled=True)
        return arrived.reshape(2, rows, columns)

    z_shape, g_shape = f32((2, EPOCHS) + fold), f32((2, pairs) + fold)
    tables = [
        pltpu.VMEM((2 * pairs + 1, 2) + fold, jnp.float32),
        pltpu.VMEM((EPOCHS + 1, 2) + fold, jnp.float32),
    ]
    small = [smem_spec()] * 3
    z, g, predicted = pl.pallas_call(
        invert_first_kernel,
        out_shape=(z_shape, g_shape, g_shape),
        in_specs=small + [vmem_spec()],
        out_specs=(vmem_spec(),) * 3,
        scratch_shapes=tables + [tables[1]],
        compiler_params=params(),
        name="invert_first",
    )(coef, seg, ends, spread(motion))
    motion = pl.pallas_call(
        again_kernel,
        out_shape=f32((2, rows, columns)),
        in_specs=[smem_spec()] + [vmem_spec()] * 3,
        out_specs=vmem_spec(),
        scratch_shapes=weight_scratch(steps, columns),
        compiler_params=params(),
        name="match_again",
    )(offsets, e, prior, collect(predicted))
    z, g = pl.pallas_call(
        invert_last_kernel,
        out_shape=(z_shape, g_shape),
        in_specs=small + [vmem_spec()] * 3,
        out_specs=(vmem_spec(),) * 2,
        scratch_shapes=tables,
        compiler_params=params(),
        name="invert_last",
    )(coef, seg, ends, spread(motion), z, g)
    return (z.reshape(2, EPOCHS, 1, pixels), motion[:, None])


def solution(mesh):
    placed = (
        P(("groups", "pairs"), "rows", None),
        P(("groups", "pairs"), "rows", None),
        P(None, ("groups", "pairs"), "rows", None),
        P(),
        P("groups", None),
        P("groups"),
    )
    return jax.shard_map(
        per_device,
        mesh=mesh,
        in_specs=placed,
        out_specs=(
            P(None, None, ("groups", "rows"), "pairs"),
            P(None, ("groups", "pairs"), "rows", None),
        ),
        check_vma=False,
    )
```

profile of v0, /device:TPU:0, one launch (start us, length us, event | category | flops | bytes accessed | tf_op | source)
XLA Modules:
  0.0 41.7 jit_solution(2092570579077779490)
XLA Ops:
  0.6 0.8 %copy.9.epochs_ref = s32[8,2]{1,0:T(8,128)S(1)} copy(s32[8,2]{0,1:T(2,128)} %param.10) | data formatting | bytes 128 | tf_op args[4]
  1.4 0.8 %copy.8.offsets_ref = s32[64,2]{1,0:T(8,128)S(1)} copy(s32[64,2]{0,1:T(2,128)} %param.9) | data formatting | bytes 1024 | tf_op args[3]
  2.2 0.0 copy-start
  2.2 0.9 %copy-done = f32[2,1,64,256]{3,2,1,0:T(8,128)S(1)} copy-done((f32[2,1,64,256]{3,2,1,0:T(8,128)S(1)}, f32[2,1,64,256]{3,2,1,0:T(8,128)}, u32[]{:S(2)}) %copy-start) | copy-done | bytes 131096
  3.1 0.0 copy-start.1
  3.1 0.8 %copy-done.1 = f32[1,64,256]{2,1,0:T(8,128)S(1)} copy-done((f32[1,64,256]{2,1,0:T(8,128)S(1)}, f32[1,64,256]{2,1,0:T(8,128)}, u32[]{:S(2)}) %copy-start.1) | copy-done | bytes 65560
  3.9 0.0 copy-start.2
  3.9 0.8 %copy-done.2 = f32[1,64,256]{2,1,0:T(8,128)S(1)} copy-done((f32[1,64,256]{2,1,0:T(8,128)S(1)}, f32[1,64,256]{2,1,0:T(8,128)}, u32[]{:S(2)}) %copy-start.2) | copy-done | bytes 65560
  4.7 0.0 copy-start.3
  4.7 0.7 %copy-done.3 = s32[8]{0:T(128)S(1)} copy-done((s32[8]{0:T(128)S(1)}, s32[8]{0:T(128)}, u32[]{:S(2)}) %copy-start.3) | copy-done | bytes 56
  5.4 34.3 %track.1 = (f32[2,128,16,128]{3,2,1,0:T(8,128)S(1)}, f32[2,64,256]{2,1,0:T(8,128)S(1)}) custom-call(s32[64,2]{1,0:T(8,128)S(1)} %copy.8.offsets_ref, s32[8,2]{1,0:T(8,128)S(1)} %copy.9.epochs_ref, s32[8]{0:T(128)S(1)} %copy-done.3, f32[64,256]{1,0:T(8,128)S(1)} %bitcast.10, f32[64,256]{1,0:T(8,128)S(1)} %bitcast.11, f32[2,64,256]{2,1,0:T(8,128)S(1)} %bitcast.8), custom_call_target="tpu_custom_call" | custom-call | tf_op jit(solution)/shard_map/track/pallas_call | solution.py:640
  39.7 1.3 %copy.14 = f32[2,128,1,2048]{3,2,1,0:T(1,128)} copy(f32[2,128,1,2048]{3,2,1,0:T(1,128)S(1)} %bitcast.7) | data formatting | bytes 4194304
  41.0 0.7 %copy.15 = f32[2,1,64,256]{3,2,1,0:T(8,128)} copy(f32[2,1,64,256]{3,2,1,0:T(8,128)S(1)} %bitcast.9) | data formatting | bytes 262144
Async XLA Ops:
  2.2 0.9 %copy-start = (f32[2,1,64,256]{3,2,1,0:T(8,128)S(1)}, f32[2,1,64,256]{3,2,1,0:T(8,128)}, u32[]{:S(2)}) copy-start(f32[2,1,64,256]{3,2,1,0:T(8,128)} %param.8) | copy-start | bytes 393220
  3.1 0.8 %copy-start.1 = (f32[1,64,256]{2,1,0:T(8,128)S(1)}, f32[1,64,256]{2,1,0:T(8,128)}, u32[]{:S(2)}) copy-start(f32[1,64,256]{2,1,0:T(8,128)} %param.6) | copy-start | bytes 196612
  3.9 0.8 %copy-start.2 = (f32[1,64,256]{2,1,0:T(8,128)S(1)}, f32[1,64,256]{2,1,0:T(8,128)}, u32[]{:S(2)}) copy-start(f32[1,64,256]{2,1,0:T(8,128)} %param.7) | copy-start | bytes 196612
  4.7 0.7 %copy-start.3 = (s32[8]{0:T(128)S(1)}, s32[8]{0:T(128)}, u32[]{:S(2)}) copy-start(s32[8]{0:T(128)} %slot_ref.1) | copy-start | bytes 100
where the time goes:
time: 42 us; the launch traced here: 41.7 us
  Pallas kernels  34.3 us (82%)
  local copies, waits for them, and re-layouts  6.73 us (16%)
  between operations  0.64 us (2%)
    pallas_call x1, Pallas kernels, fused(): pl.pallas_call(fused_kernel, out_shape=(jax.ShapeDtypeStruct((2, EPOCHS,...  34.3 us
    unnamed x12, local copies, waits for them, and re-layouts  6.73 us

commit v1 on v0

--- a/solution.py
+++ b/solution.py
@@ -141,26 +141,23 @@
         inv_ref[place] = inv.reshape(wide, SUB, columns)
 
 
-def correlate(offsets_ref, f_ref, s_ref, mean_ref, inv_ref, mean1_ref, inv1_ref, e_ref):
+def correlate(shift, count, f_ref, s_ref, mean_ref, inv_ref, mean1_ref, inv1_ref, e_ref):
     steps, _, columns = mean1_ref.shape
     rows = steps * SUB
     band = band_matrix(columns, 0)
-    count = offsets_ref.shape[0]
     block = BLOCK if count % BLOCK == 0 else 1
 
     def body(number, carry):
         sums = []
         for i in range(block):
             k = number * block + i
-            oy = offsets_ref[k, 0] + SEARCH
-            ox = offsets_ref[k, 1] + SEARCH
+            oy, ox = shift(k)
             planes = [f_ref[t] * s_ref[ox, oy + t] for t in range(steps + 2 * RADIUS)]
             sums += row_box(planes, steps)
         boxed = column_box(jnp.concatenate(sums, axis=0), band)
         for i in range(block):
             k = number * block + i
-            oy = offsets_ref[k, 0] + SEARCH
-            ox = offsets_ref[k, 1] + SEARCH
+            oy, ox = shift(k)
             for t in range(steps):
                 at = i * rows + t * SUB
                 cov = boxed[at : at + SUB] - mean1_ref[t] * mean_ref[ox, oy + t]
@@ -205,7 +202,33 @@
             store(base + i, rows[i] / total[i], cols[i] / total[i])
 
 
-def design_kernel(epochs_ref, slot_ref, coef_ref, seg_ref, ends_ref):
+def match_cells(cell, e_ref, a_ref, b_ref, lanes, together, store):
+    steps = e_ref.shape[1]
+    for base in range(0, steps, together):
+        here = pl.ds(base, together)
+        zero = jnp.zeros((together, SUB, lanes.size), jnp.float32)
+        table = [b_ref[j, here, :, lanes] for j in range(SIDE)]
+        moment = [x * float(j - SEARCH) for j, x in enumerate(table)]
+
+        def body(i, carry):
+            total, rows, cols = carry
+            first, second = zero, zero
+            for j in range(SIDE):
+                e = e_ref[cell(i * SIDE + j), here, :, lanes]
+                first = first + e * table[j]
+                if j != SEARCH:
+                    second = second + e * moment[j]
+            a = a_ref[i, here, :, lanes]
+            weight = a * first
+            shift = lax.convert_element_type(i - SEARCH, jnp.float32)
+            return total + weight, rows + weight * shift, cols + a * second
+
+        total, rows, cols = lax.fori_loop(0, SIDE, body, (zero, zero, zero), unroll=True)
+        for i in range(together):
+            store(base + i, rows[i] / total[i], cols[i] / total[i])
+
+
+def design_kernel(epochs_ref, slot_ref, coef_ref, seg_ref, ends_ref, weigh=False):
     pairs = slot_ref.shape[0]
     ends = 2 * pairs
     row_id = lax.broadcasted_iota(jnp.int32, (pairs, pairs), 0)
@@ -217,10 +240,11 @@
 
     def gather(j, state):
         first_r, after_r, first_c, after_c, mark, mark_e, first_e, after_e = state
-        first = epochs_ref[slot_ref[j], 0]
-        after = epochs_ref[slot_ref[j], 1]
-        ends_ref[0, j] = first
-        ends_ref[1, j] = after
+        first = epochs_ref[0, slot_ref[j]]
+        after = epochs_ref[1, slot_ref[j]]
+        if ends_ref is not None:
+            ends_ref[0, j] = first
+            ends_ref[1, j] = after
         return (
             jnp.where(row_id == j, first, first_r),
             jnp.where(row_id == j, after, after_r),
@@ -257,14 +281,16 @@
 
     inverse = lax.fori_loop(0, pairs, eliminate, matrix)
     inside = ((mark >= first_e) & (mark < after_e)).astype(jnp.float32)
-    coef = jnp.dot(inside, inverse, precision=HIGHEST, preferred_element_type=jnp.float32)
-    wider = coef_ref.shape[1] - pairs
-    if wider:
-        coef = jnp.concatenate([coef, jnp.zeros((ends, wider), jnp.float32)], axis=1)
-    coef_ref[...] = coef
     latest = jnp.max(jnp.where(mark_e <= epoch, mark_e, -1), axis=0, keepdims=True)
     which = jnp.max(jnp.where(mark_e == latest, seg_id, -1), axis=0, keepdims=True)
-    seg_ref[...] = jnp.broadcast_to(jnp.where(latest < 0, ends, which), seg_ref.shape)
+    which = jnp.where(latest < 0, ends, which)
+    seg_ref[0:1] = which
+    coef = jnp.dot(inside, inverse, precision=HIGHEST, preferred_element_type=jnp.float32)
+    if weigh:
+        long = jnp.sum((which == seg_id).astype(jnp.float32), axis=1, keepdims=True)
+        blank = jnp.zeros((ends, coef_ref.shape[1] - ends), jnp.float32)
+        coef = jnp.concatenate([coef, inside * long, blank], axis=1)
+    coef_ref[...] = coef
 
 
 def design(pair_epochs, pair_slot):
@@ -280,7 +306,7 @@
         out_specs=(vmem_spec(), vmem_spec(), smem_spec()),
         compiler_params=params(),
         name="design",
-    )(pair_epochs, pair_slot)
+    )(pair_epochs.T, pair_slot)
 
 
 def invert(coef_ref, seg_ref, ends_ref, pairs, d, begin, z, g, t_ref, cum_ref, predict):
@@ -352,6 +378,44 @@
             pl.loop(0, pairs)(collect)
 
 
+def invert_segments(coef_ref, pairs, d, z_ref, g_ref, fresh):
+    ends = 2 * pairs
+    threshold = SPARSITY / PENALTY
+    zero = jnp.zeros(z_ref.shape[1:], jnp.float32)
+    if fresh:
+        for j in range(ends + 1):
+            z_ref[j] = zero
+    seen = [d(p) for p in range(pairs)]
+
+    def weigh(j, value, sums):
+        return tuple(g + coef_ref[j, pairs + p] * value for p, g in enumerate(sums))
+
+    def step(iteration, held):
+        gaps = [a - b for a, b in zip(seen, held)]
+        sums = (zero,) * pairs
+        for j in range(ends):
+            terms = [coef_ref[j, p] * gap for p, gap in enumerate(gaps)]
+            while len(terms) > 1:
+                terms = [sum(terms[i : i + 2][1:], terms[i]) for i in range(0, len(terms), 2)]
+            s = z_ref[j] + terms[0]
+            u = jnp.clip(s, -threshold, threshold)
+            z = s - u
+            z_ref[j] = z
+            sums = weigh(j, z - u, sums)
+        return sums
+
+    held = (zero,) * pairs if fresh else tuple(g_ref[p] for p in range(pairs))
+    held = lax.fori_loop(0, ITERS, step, held)
+    if not fresh:
+        return None
+    for p in range(pairs):
+        g_ref[p] = held[p]
+    sums = (zero,) * pairs
+    for j in range(ends):
+        sums = weigh(j, z_ref[j], sums)
+    return sums
+
+
 def second_axis(ref):
     def store(i, value, last=False):
         ref[:, i] = value
@@ -406,7 +470,8 @@
     for i in range(2):
         image_ref[i] = split_lanes(images_ref[i])
     prepare(image_ref, *tables)
-    correlate(offsets_ref, *tables, e_ref)
+    shift = lambda k: (offsets_ref[k, 0] + SEARCH, offsets_ref[k, 1] + SEARCH)
+    correlate(shift, offsets_ref.shape[0], *tables, e_ref)
     match_on(offsets_ref, e_ref, prior_ref, None, *scratch[7:], motion_ref)
 
 
@@ -428,12 +493,12 @@
 
 
 def fused_kernel(
-    offsets_ref,
-    epochs_ref,
-    slot_ref,
-    first_ref,
-    second_ref,
-    prior_ref,
+    offsets_hbm,
+    epochs_hbm,
+    slot_hbm,
+    first_hbm,
+    second_hbm,
+    prior_hbm,
     velocity_ref,
     motion_ref,
     image_ref,
@@ -447,32 +512,31 @@
     b_ref,
     field_ref,
     e_ref,
-    prior_split_ref,
+    prior_ref,
     back_ref,
-    edge_ref,
-    halo_ref,
     d_ref,
     gz_ref,
     z_ref,
     g_ref,
-    t_ref,
-    cum_ref,
-    cumz_ref,
     coef_vmem,
-    seg_vmem,
+    index_vmem,
     coef_ref,
-    seg_ref,
-    ends_ref,
+    index_ref,
+    offsets_ref,
+    epochs_ref,
+    slot_ref,
+    load_sem,
     table_sem,
     halo_sem,
     send_sem,
     recv_sem,
 ):
-    rows, columns = first_ref.shape
+    rows, columns = first_hbm.shape
     steps = rows // SUB
     halves = columns // LANES
     pairs = slot_ref.shape[0]
     part = rows // pairs
+    count = offsets_ref.shape[1]
     me = lax.axis_index("pairs")
     band = lax.axis_index("rows")
     mesh_id = pl.DeviceIdType.MESH
@@ -482,48 +546,75 @@
     pl.semaphore_signal(barrier, inc=1, device_id={"rows": 1 - band}, device_id_type=mesh_id)
     for peer in peers:
         pl.semaphore_signal(barrier, inc=1, device_id={"pairs": peer}, device_id_type=mesh_id)
+
+    moves = [(epochs_hbm, epochs_ref), (slot_hbm, slot_ref), (offsets_hbm, offsets_ref)]
+    for half in range(halves):
+        lanes = pl.ds(half * LANES, LANES)
+        inner = pl.ds(MARGIN, rows)
+        moves += [
+            (prior_hbm.at[0, :, lanes], prior_ref.at[0, half]),
+            (prior_hbm.at[1, :, lanes], prior_ref.at[1, half]),
+            (first_hbm.at[:, lanes], image_ref.at[0, half, inner]),
+            (second_hbm.at[:, lanes], image_ref.at[1, half, inner]),
+        ]
+    loads = [
+        pltpu.make_async_copy(source, target, load_sem.at[i])
+        for i, (source, target) in enumerate(moves)
+    ]
+    for load in loads:
+        load.start()
+    outer = pl.ds(pl.multiple_of(band * (rows + MARGIN), SUB), MARGIN)
     edge = pl.ds(pl.multiple_of((1 - band) * (rows - MARGIN), SUB), MARGIN)
-    edge_ref[0] = first_ref[edge, :]
-    edge_ref[1] = second_ref[edge, :]
+    image_ref[:, :, outer, :] = jnp.zeros((2, halves, MARGIN, LANES), jnp.float32)
     pl.semaphore_wait(barrier, pairs)
-    halo = pltpu.make_async_remote_copy(
-        src_ref=edge_ref,
-        dst_ref=halo_ref,
-        send_sem=halo_sem.at[0],
-        recv_sem=halo_sem.at[1],
-        device_id={"rows": 1 - band},
-        device_id_type=mesh_id,
-    )
-    halo.start()
-
-    design_kernel(epochs_ref, slot_ref, coef_vmem, seg_vmem, ends_ref)
-    moves = [
+    halos = []
+    for i, source in enumerate((first_hbm, second_hbm)):
+        for half in range(halves):
+            halo = pltpu.make_async_remote_copy(
+                src_ref=source.at[edge, pl.ds(half * LANES, LANES)],
+                dst_ref=image_ref.at[i, half, outer, :],
+                send_sem=halo_sem.at[0, i, half],
+                recv_sem=halo_sem.at[1, i, half],
+                device_id={"rows": 1 - band},
+                device_id_type=mesh_id,
+            )
+            halo.start()
+            halos.append(halo)
+
+    for load in loads[:3]:
+        load.wait()
+    index_vmem[...] = jnp.zeros(index_vmem.shape, jnp.int32)
+    design_kernel(epochs_ref, slot_ref, coef_vmem, index_vmem, None, True)
+    lane = lax.broadcasted_iota(jnp.int32, (1, LANES), 1)
+
+    def place(k, held):
+        cell = (offsets_ref[0, k] + SEARCH) * SIDE + offsets_ref[1, k] + SEARCH
+        return jnp.where(lane == cell, k, held)
+
+    index_vmem[1:2] = lax.fori_loop(0, count, place, jnp.full((1, LANES), count, jnp.int32), unroll=8)
+    tables = [
         pltpu.make_async_copy(coef_vmem, coef_ref, table_sem.at[0]),
-        pltpu.make_async_copy(seg_vmem, seg_ref, table_sem.at[1]),
+        pltpu.make_async_copy(index_vmem, index_ref, table_sem.at[1]),
     ]
-    for move in moves:
+    for move in tables:
         move.start()
-    everywhere = pl.ds(0, columns)
-    for component in range(2):
-        prior_split_ref[component] = split_lanes(prior_ref[component])
+    e_ref[count] = jnp.zeros(e_ref.shape[1:], jnp.float32)
+    for load in loads[3:]:
+        load.wait()
     prior_tables(
-        lambda t: strided(prior_split_ref.at[0], t, steps),
-        lambda t: strided(prior_split_ref.at[1], t, steps),
+        lambda t: strided(prior_ref.at[0], t, steps),
+        lambda t: strided(prior_ref.at[1], t, steps),
         a_ref,
         b_ref,
-        everywhere,
+        pl.ds(0, columns),
     )
-    for i, ref in enumerate((first_ref, second_ref)):
-        image_ref[i, :, MARGIN : MARGIN + rows, :] = split_lanes(ref[...])
-    halo.wait()
-    for i in range(2):
-        arrived = split_lanes(halo_ref[i])
-        image_ref[i, :, :MARGIN, :] = jnp.where(band == 1, arrived, 0.0)
-        image_ref[i, :, MARGIN + rows :, :] = jnp.where(band == 0, arrived, 0.0)
-    for move in moves:
+    for halo in halos:
+        halo.wait()
+    for move in tables:
         move.wait()
     prepare(image_ref, f_ref, s_ref, mean_ref, inv_ref, mean1_ref, inv1_ref)
-    correlate(offsets_ref, f_ref, s_ref, mean_ref, inv_ref, mean1_ref, inv1_ref, e_ref)
+    shift = lambda k: (offsets_ref[0, k] + SEARCH, offsets_ref[1, k] + SEARCH)
+    correlate(shift, count, f_ref, s_ref, mean_ref, inv_ref, mean1_ref, inv1_ref, e_ref)
 
     def block(index):
         return pl.ds(pl.multiple_of(index * part, SUB), part)
@@ -555,7 +646,8 @@
             field_ref[0, half, pl.ds(t, SUB, stride=steps), :] = row
             field_ref[1, half, pl.ds(t, SUB, stride=steps), :] = col
 
-        match(offsets_ref, e_ref, a_ref, b_ref, lanes, 4 if steps % 4 == 0 else 1, store)
+        cell = lambda i: index_ref[1, i]
+        match_cells(cell, e_ref, a_ref, b_ref, lanes, 2 if steps % 2 == 0 else 1, store)
         return push(
             phase,
             half,
@@ -564,35 +656,27 @@
         )
 
     def invert_half(phase, half):
-        def store_z(e, value, last):
-            if phase and last:
-                for component in range(2):
-                    place = pl.ds(half, part, stride=halves)
-                    velocity_ref[component, e, place, :] = value[component]
-            else:
-                z_ref[half, e] = value
-
-        def store_g(p, value):
-            g_ref[half, p] = value
-
-        def store_gz(p, value):
-            gz_ref[half, p] = value
-
-        z = ((lambda e: z_ref[half, e]), store_z)
-        g = ((lambda p: g_ref[half, p]), store_g)
-        invert(
+        sums = invert_segments(
             coef_ref,
-            seg_ref,
-            ends_ref,
             pairs,
             lambda p: d_ref[phase // 2, half, p],
-            (z[0], g[0]) if phase else None,
-            z,
-            g,
-            t_ref,
-            cum_ref,
-            None if phase else (store_gz, cumz_ref),
+            z_ref.at[half],
+            g_ref.at[half],
+            phase == 0,
         )
+        if phase == 0:
+            for p in range(pairs):
+                gz_ref[half, p] = sums[p]
+            return
+
+        def expand(e, carry):
+            plane = z_ref[half, index_ref[0, e]]
+            for component in range(2):
+                rows_of = pl.ds(half, part, stride=halves)
+                velocity_ref[component, e, rows_of, :] = plane[component]
+            return carry
+
+        lax.fori_loop(0, EPOCHS, expand, 0, unroll=8)
 
     sent = [match_half(0, half) for half in range(halves)]
     returned = []
@@ -614,7 +698,7 @@
         def prior(component):
             def at(t):
                 place = pl.ds(t, SUB, stride=steps)
-                given = prior_split_ref[component, half, place, :]
+                given = prior_ref[component, half, place, :]
                 return 0.5 * (given + back_ref[component, half, place, :])
 
             return at
@@ -632,47 +716,46 @@
 def fused(first_image, second_image, prior, offsets, pair_epochs, pair_slot):
     rows, columns = first_image.shape
     steps, halves = rows // SUB, columns // LANES
-    pairs = pair_slot.shape[0]
+    count, pairs = offsets.shape[0], pair_slot.shape[0]
     part = rows // pairs
-    f32 = jnp.float32
+    f32, i32 = jnp.float32, jnp.int32
     plane = (2, part, LANES)
     split = (2, halves, rows, LANES)
+    dma = pltpu.SemaphoreType.DMA
     return pl.pallas_call(
         fused_kernel,
         out_shape=(
             jax.ShapeDtypeStruct((2, EPOCHS, part * halves, LANES), f32),
             jax.ShapeDtypeStruct((2, rows, columns), f32),
         ),
-        in_specs=[smem_spec()] * 3 + [vmem_spec()] * 3,
+        in_specs=[pl.BlockSpec(memory_space=pltpu.HBM)] * 6,
         out_specs=(vmem_spec(), vmem_spec()),
         scratch_shapes=match_scratch(steps, columns)
         + weight_scratch(steps, columns)
         + [
-            pltpu.VMEM((offsets.shape[0], steps, SUB, columns), f32),
+            pltpu.VMEM((count + 1, steps, SUB, columns), f32),
             pltpu.VMEM(split, f32),
             pltpu.VMEM(split, f32),
-            pltpu.VMEM((2, MARGIN, columns), f32),
-            pltpu.VMEM((2, MARGIN, columns), f32),
             pltpu.VMEM((ROUNDS, halves, pairs) + plane, f32),
             pltpu.VMEM((halves, pairs) + plane, f32),
-            pltpu.VMEM((halves, EPOCHS) + plane, f32),
+            pltpu.VMEM((halves, 2 * pairs + 1) + plane, f32),
             pltpu.VMEM((halves, pairs) + plane, f32),
-            pltpu.VMEM((2 * pairs + 1,) + plane, f32),
-            pltpu.VMEM((EPOCHS + 1,) + plane, f32),
-            pltpu.VMEM((EPOCHS + 1,) + plane, f32),
             pltpu.VMEM((2 * pairs, LANES), f32),
-            pltpu.VMEM((SUB, EPOCHS), jnp.int32),
+            pltpu.VMEM((SUB, EPOCHS), i32),
             pltpu.SMEM((2 * pairs, LANES), f32),
-            pltpu.SMEM((SUB, EPOCHS), jnp.int32),
-            pltpu.SMEM((2, pairs), jnp.int32),
-            pltpu.SemaphoreType.DMA((2,)),
-            pltpu.SemaphoreType.DMA((2,)),
-            pltpu.SemaphoreType.DMA((3, halves, pairs)),
-            pltpu.SemaphoreType.DMA((3, halves, pairs)),
+            pltpu.SMEM((SUB, EPOCHS), i32),
+            pltpu.SMEM((2, count), i32),
+            pltpu.SMEM((2, pairs), i32),
+            pltpu.SMEM((pairs,), i32),
+            dma((3 + 4 * halves,)),
+            dma((2,)),
+            dma((2, 2, halves)),
+            dma((3, halves, pairs)),
+            dma((3, halves, pairs)),
         ],
         compiler_params=params(collective_id=0, has_side_effects=True),
         name="track",
-    )(offsets, pair_epochs, pair_slot, first_image, second_image, prior)
+    )(offsets.T, pair_epochs.T, pair_slot, first_image, second_image, prior)
 
 
 def with_halo(cells, axis, dim, width):
@@ -692,7 +775,7 @@
     fold = (pixels // LANES, LANES) if pixels % LANES == 0 else (1, pixels)
     f32 = functools.partial(jax.ShapeDtypeStruct, dtype=jnp.float32)
     prior = prior_motion[:, 0]
-    whole_tiles = rows % (SUB * pairs) == 0 and columns % LANES == 0 and pairs <= LANES
+    whole_tiles = rows % (SUB * pairs) == 0 and columns % LANES == 0 and 2 * pairs <= LANES
     if whole_tiles and lax.axis_size("rows") == 2:
         velocity, motion = fused(
             first_image[0], second_image[0], prior, offsets, pair_epochs, pair_slot

time: 42 us -> 38.4 us (0.914)
  Pallas kernels: 34.3 us -> 30.9 us
    pallas_call x1, Pallas kernels: 34.3 us -> 30.9 us  [fused(): pl.pallas_call(fused_kernel, out_shape=(jax.ShapeDtypeStruct((2, EPOCHS,...]
    unnamed x12 -> x14, local copies, waits for them, and re-layouts: 6.73 us -> 6.56 us
where the time goes in v1:
time: 38.4 us; the launch traced here: 38.1 us
  Pallas kernels  30.9 us (80%)
  local copies, waits for them, and re-layouts  6.56 us (17%)
  between operations  0.65 us (2%)
    pallas_call x1, Pallas kernels, fused(): pl.pallas_call(fused_kernel, out_shape=(jax.ShapeDtypeStruct((2, EPOCHS,...  30.9 us
    unnamed x14, local copies, waits for them, and re-layouts  6.56 us

profile of v1, /device:TPU:0, one launch (start us, length us, event | category | flops | bytes accessed | tf_op | source)
XLA Modules:
  0.0 38.1 jit_solution(12589562814569667858)
XLA Ops:
  0.6 0.0 copy-start
  0.6 0.9 %copy-done = f32[2,1,64,256]{3,2,1,0:T(8,128)S(1)} copy-done((f32[2,1,64,256]{3,2,1,0:T(8,128)S(1)}, f32[2,1,64,256]{3,2,1,0:T(8,128)}, u32[]{:S(2)}) %copy-start) | copy-done | bytes 131096
  1.5 0.0 copy-start.1
  1.5 0.8 %copy-done.1 = f32[1,64,256]{2,1,0:T(8,128)S(1)} copy-done((f32[1,64,256]{2,1,0:T(8,128)S(1)}, f32[1,64,256]{2,1,0:T(8,128)}, u32[]{:S(2)}) %copy-start.1) | copy-done | bytes 65560
  2.4 0.0 copy-start.2
  2.4 0.8 %copy-done.2 = f32[1,64,256]{2,1,0:T(8,128)S(1)} copy-done((f32[1,64,256]{2,1,0:T(8,128)S(1)}, f32[1,64,256]{2,1,0:T(8,128)}, u32[]{:S(2)}) %copy-start.2) | copy-done | bytes 65560
  3.2 0.0 copy-start.3
  3.2 0.7 %copy-done.3 = s32[64,2]{0,1:T(2,128)S(1)} copy-done((s32[64,2]{0,1:T(2,128)S(1)}, s32[64,2]{0,1:T(2,128)}, u32[]{:S(2)}) %copy-start.3) | copy-done | bytes 536
  3.9 0.0 copy-start.4
  3.9 0.7 %copy-done.4 = s32[8,2]{0,1:T(2,128)S(1)} copy-done((s32[8,2]{0,1:T(2,128)S(1)}, s32[8,2]{0,1:T(2,128)}, u32[]{:S(2)}) %copy-start.4) | copy-done | bytes 88
  4.6 0.0 copy-start.5
  4.6 0.7 %copy-done.5 = s32[8]{0:T(128)S(1)} copy-done((s32[8]{0:T(128)S(1)}, s32[8]{0:T(128)}, u32[]{:S(2)}) %copy-start.5) | copy-done | bytes 56
  5.2 30.9 %track.1 = (f32[2,128,16,128]{3,2,1,0:T(8,128)S(1)}, f32[2,64,256]{2,1,0:T(8,128)S(1)}) custom-call(s32[2,64]{1,0:T(2,128)S(1)} %bitcast.14, s32[2,8]{1,0:T(2,128)S(1)} %bitcast.15, s32[8]{0:T(128)S(1)} %copy-done.5, f32[64,256]{1,0:T(8,128)S(1)} %bitcast.12, f32[64,256]{1,0:T(8,128)S(1)} %bitcast.13, f32[2,64,256]{2,1,0:T(8,128)S(1)} %bitcast.10), custom_call_target="tpu_custom_call" | custom-call | tf_op jit(solution)/shard_map/track/pallas_call | solution.py:725
  36.1 1.3 %copy.12 = f32[2,128,1,2048]{3,2,1,0:T(1,128)} copy(f32[2,128,1,2048]{3,2,1,0:T(1,128)S(1)} %bitcast.9) | data formatting | bytes 4194304
  37.5 0.7 %copy.13 = f32[2,1,64,256]{3,2,1,0:T(8,128)} copy(f32[2,1,64,256]{3,2,1,0:T(8,128)S(1)} %bitcast.11) | data formatting | bytes 262144
Async XLA Ops:
  0.6 0.9 %copy-start = (f32[2,1,64,256]{3,2,1,0:T(8,128)S(1)}, f32[2,1,64,256]{3,2,1,0:T(8,128)}, u32[]{:S(2)}) copy-start(f32[2,1,64,256]{3,2,1,0:T(8,128)} %param.8) | copy-start | bytes 393220
  1.5 0.8 %copy-start.1 = (f32[1,64,256]{2,1,0:T(8,128)S(1)}, f32[1,64,256]{2,1,0:T(8,128)}, u32[]{:S(2)}) copy-start(f32[1,64,256]{2,1,0:T(8,128)} %param.6) | copy-start | bytes 196612
  2.4 0.8 %copy-start.2 = (f32[1,64,256]{2,1,0:T(8,128)S(1)}, f32[1,64,256]{2,1,0:T(8,128)}, u32[]{:S(2)}) copy-start(f32[1,64,256]{2,1,0:T(8,128)} %param.7) | copy-start | bytes 196612
  3.2 0.7 %copy-start.3 = (s32[64,2]{0,1:T(2,128)S(1)}, s32[64,2]{0,1:T(2,128)}, u32[]{:S(2)}) copy-start(s32[64,2]{0,1:T(2,128)} %param.9) | copy-start | bytes 1540
  3.9 0.7 %copy-start.4 = (s32[8,2]{0,1:T(2,128)S(1)}, s32[8,2]{0,1:T(2,128)}, u32[]{:S(2)}) copy-start(s32[8,2]{0,1:T(2,128)} %param.10) | copy-start | bytes 196
  4.6 0.7 %copy-start.5 = (s32[8]{0:T(128)S(1)}, s32[8]{0:T(128)}, u32[]{:S(2)}) copy-start(s32[8]{0:T(128)} %slot_hbm.1) | copy-start | bytes 100

commit v2 on v1

--- a/solution.py
+++ b/solution.py
@@ -26,8 +26,9 @@
 SUB = 8
 LANES = 128
 AREA = 1.0 / float(WINDOW * WINDOW)
-VMEM_BYTES = 40 * 1024 * 1024
+VMEM_BYTES = 64 * 1024 * 1024
 BLOCK = 4
+PIECES = 4
 
 
 def vmem_spec():
@@ -36,6 +37,10 @@
 
 def smem_spec():
     return pl.BlockSpec(memory_space=pltpu.SMEM)
+
+
+def hbm_spec():
+    return pl.BlockSpec(memory_space=pltpu.HBM)
 
 
 def params(**more):
@@ -57,9 +62,9 @@
 
 
 def column_box(values, band):
-    high, middle, low = parts_of(values)
-    mm = functools.partial(jnp.dot, preferred_element_type=jnp.float32)
-    return mm(high, band) + (mm(middle, band) + mm(low, band))
+    parts = jnp.concatenate(parts_of(values), axis=1)
+    bands = jnp.concatenate([band] * 3, axis=0)
+    return jnp.dot(parts, bands, preferred_element_type=jnp.float32)
 
 
 def row_box(planes, count):
@@ -119,7 +124,7 @@
     second = [strided(image_ref.at[1], t, steps) for t in range(reach)]
     wide = steps + 2 * SEARCH
     sums = row_box(second, wide) + row_box([x * x for x in second], wide)
-    sums = parts_of(jnp.concatenate(sums, axis=0))
+    sums = jnp.concatenate(parts_of(jnp.concatenate(sums, axis=0)), axis=1)
     stacked = jnp.concatenate(second, axis=0)
     lane = lax.broadcasted_iota(jnp.int32, stacked.shape, 1)
     half = wide * SUB
@@ -129,11 +134,8 @@
         inside = (lane + shift >= 0) & (lane + shift < columns)
         s_ref[place] = jnp.where(inside, moved, 0.0).reshape(reach, SUB, columns)
         shifted_band = band_matrix(columns, shift)
-        mm = functools.partial(jnp.dot, preferred_element_type=jnp.float32)
-        boxed = mm(sums[0], shifted_band) + (
-            mm(sums[1], shifted_band) + mm(sums[2], shifted_band)
-        )
-        boxed = boxed * AREA
+        bands = jnp.concatenate([shifted_band] * 3, axis=0)
+        boxed = jnp.dot(sums, bands, preferred_element_type=jnp.float32) * AREA
         mean = boxed[:half]
         var = boxed[half:] - mean * mean
         mean_ref[place] = mean.reshape(wide, SUB, columns)
@@ -141,7 +143,7 @@
         inv_ref[place] = inv.reshape(wide, SUB, columns)
 
 
-def correlate(shift, count, f_ref, s_ref, mean_ref, inv_ref, mean1_ref, inv1_ref, e_ref):
+def correlate(shift, count, f_ref, s_ref, mean_ref, inv_ref, mean1_ref, inv1_ref, e_ref, side=None, held=None):
     steps, _, columns = mean1_ref.shape
     rows = steps * SUB
     band = band_matrix(columns, 0)
@@ -162,9 +164,9 @@
                 at = i * rows + t * SUB
                 cov = boxed[at : at + SUB] - mean1_ref[t] * mean_ref[ox, oy + t]
                 e_ref[k, t] = jnp.exp(cov * (inv1_ref[t] * inv_ref[ox, oy + t]))
-        return carry
-
-    lax.fori_loop(0, count // block, body, 0)
+        return carry if side is None else side(number, carry)
+
+    return count // block, lax.fori_loop(0, count // block, body, 0 if side is None else held)
 
 
 def prior_tables(prior_row, prior_col, a_ref, b_ref, lanes):
@@ -228,7 +230,24 @@
             store(base + i, rows[i] / total[i], cols[i] / total[i])
 
 
-def design_kernel(epochs_ref, slot_ref, coef_ref, seg_ref, ends_ref, weigh=False):
+def eliminate(j, a):
+    row_id = lax.broadcasted_iota(jnp.int32, a.shape, 0)
+    col_id = lax.broadcasted_iota(jnp.int32, a.shape, 1)
+    on_row = row_id == j
+    on_col = col_id == j
+    row = jnp.sum(jnp.where(on_row, a, 0.0), axis=0, keepdims=True)
+    col = jnp.sum(jnp.where(on_col, a, 0.0), axis=1, keepdims=True)
+    pivot = jnp.sum(jnp.where(col_id[:1] == j, row, 0.0), axis=1, keepdims=True)
+    scale = jnp.where(j < a.shape[0], 1.0 / pivot, 0.0)
+    inner = a - col * (row * scale)
+    return jnp.where(
+        on_row,
+        jnp.where(on_col, scale, row * scale),
+        jnp.where(on_col, -col * scale, inner),
+    )
+
+
+def design_begin(epochs_ref, slot_ref, ends_ref):
     pairs = slot_ref.shape[0]
     ends = 2 * pairs
     row_id = lax.broadcasted_iota(jnp.int32, (pairs, pairs), 0)
@@ -236,7 +255,6 @@
     end_id = lax.broadcasted_iota(jnp.int32, (ends, pairs), 0)
     end_col = lax.broadcasted_iota(jnp.int32, (ends, pairs), 1)
     seg_id = lax.broadcasted_iota(jnp.int32, (ends, EPOCHS), 0)
-    epoch = lax.broadcasted_iota(jnp.int32, (ends, EPOCHS), 1)
 
     def gather(j, state):
         first_r, after_r, first_c, after_c, mark, mark_e, first_e, after_e = state
@@ -265,22 +283,15 @@
     overlap = jnp.maximum(jnp.minimum(after_r, after_c) - jnp.maximum(first_r, first_c), 0)
     matrix = overlap.astype(jnp.float32) + jnp.where(row_id == col_id, PENALTY, 0.0)
 
-    def eliminate(j, a):
-        on_row = row_id == j
-        on_col = col_id == j
-        row = jnp.sum(jnp.where(on_row, a, 0.0), axis=0, keepdims=True)
-        col = jnp.sum(jnp.where(on_col, a, 0.0), axis=1, keepdims=True)
-        pivot = jnp.sum(jnp.where(col_id[:1] == j, row, 0.0), axis=1, keepdims=True)
-        scale = 1.0 / pivot
-        inner = a - col * (row * scale)
-        return jnp.where(
-            on_row,
-            jnp.where(on_col, scale, row * scale),
-            jnp.where(on_col, -col * scale, inner),
-        )
-
-    inverse = lax.fori_loop(0, pairs, eliminate, matrix)
     inside = ((mark >= first_e) & (mark < after_e)).astype(jnp.float32)
+    return matrix, (inside, mark_e)
+
+
+def design_end(inverse, intervals, coef_ref, seg_ref, weigh=False):
+    inside, mark_e = intervals
+    ends = inside.shape[0]
+    seg_id = lax.broadcasted_iota(jnp.int32, (ends, EPOCHS), 0)
+    epoch = lax.broadcasted_iota(jnp.int32, (ends, EPOCHS), 1)
     latest = jnp.max(jnp.where(mark_e <= epoch, mark_e, -1), axis=0, keepdims=True)
     which = jnp.max(jnp.where(mark_e == latest, seg_id, -1), axis=0, keepdims=True)
     which = jnp.where(latest < 0, ends, which)
@@ -291,6 +302,12 @@
         blank = jnp.zeros((ends, coef_ref.shape[1] - ends), jnp.float32)
         coef = jnp.concatenate([coef, inside * long, blank], axis=1)
     coef_ref[...] = coef
+
+
+def design_kernel(epochs_ref, slot_ref, coef_ref, seg_ref, ends_ref):
+    matrix, intervals = design_begin(epochs_ref, slot_ref, ends_ref)
+    inverse = lax.fori_loop(0, slot_ref.shape[0], eliminate, matrix)
+    design_end(inverse, intervals, coef_ref, seg_ref)
 
 
 def design(pair_epochs, pair_slot):
@@ -499,7 +516,8 @@
     first_hbm,
     second_hbm,
     prior_hbm,
-    velocity_ref,
+    z_ref,
+    index_vmem,
     motion_ref,
     image_ref,
     f_ref,
@@ -516,10 +534,8 @@
     back_ref,
     d_ref,
     gz_ref,
-    z_ref,
     g_ref,
     coef_vmem,
-    index_vmem,
     coef_ref,
     index_ref,
     offsets_ref,
@@ -584,7 +600,7 @@
     for load in loads[:3]:
         load.wait()
     index_vmem[...] = jnp.zeros(index_vmem.shape, jnp.int32)
-    design_kernel(epochs_ref, slot_ref, coef_vmem, index_vmem, None, True)
+    matrix, intervals = design_begin(epochs_ref, slot_ref, None)
     lane = lax.broadcasted_iota(jnp.int32, (1, LANES), 1)
 
     def place(k, held):
@@ -592,12 +608,6 @@
         return jnp.where(lane == cell, k, held)
 
     index_vmem[1:2] = lax.fori_loop(0, count, place, jnp.full((1, LANES), count, jnp.int32), unroll=8)
-    tables = [
-        pltpu.make_async_copy(coef_vmem, coef_ref, table_sem.at[0]),
-        pltpu.make_async_copy(index_vmem, index_ref, table_sem.at[1]),
-    ]
-    for move in tables:
-        move.start()
     e_ref[count] = jnp.zeros(e_ref.shape[1:], jnp.float32)
     for load in loads[3:]:
         load.wait()
@@ -610,11 +620,20 @@
     )
     for halo in halos:
         halo.wait()
+    prepare(image_ref, f_ref, s_ref, mean_ref, inv_ref, mean1_ref, inv1_ref)
+    shift = lambda k: (offsets_ref[0, k] + SEARCH, offsets_ref[1, k] + SEARCH)
+    images = (f_ref, s_ref, mean_ref, inv_ref, mean1_ref, inv1_ref)
+    done, matrix = correlate(shift, count, *images, e_ref, eliminate, matrix)
+    inverse = lax.fori_loop(done, max(done, pairs), eliminate, matrix) if done < pairs else matrix
+    design_end(inverse, intervals, coef_vmem, index_vmem, True)
+    tables = [
+        pltpu.make_async_copy(coef_vmem, coef_ref, table_sem.at[0]),
+        pltpu.make_async_copy(index_vmem, index_ref, table_sem.at[1]),
+    ]
+    for move in tables:
+        move.start()
     for move in tables:
         move.wait()
-    prepare(image_ref, f_ref, s_ref, mean_ref, inv_ref, mean1_ref, inv1_ref)
-    shift = lambda k: (offsets_ref[0, k] + SEARCH, offsets_ref[1, k] + SEARCH)
-    correlate(shift, count, f_ref, s_ref, mean_ref, inv_ref, mean1_ref, inv1_ref, e_ref)
 
     def block(index):
         return pl.ds(pl.multiple_of(index * part, SUB), part)
@@ -668,15 +687,6 @@
             for p in range(pairs):
                 gz_ref[half, p] = sums[p]
             return
-
-        def expand(e, carry):
-            plane = z_ref[half, index_ref[0, e]]
-            for component in range(2):
-                rows_of = pl.ds(half, part, stride=halves)
-                velocity_ref[component, e, rows_of, :] = plane[component]
-            return carry
-
-        lax.fori_loop(0, EPOCHS, expand, 0, unroll=8)
 
     sent = [match_half(0, half) for half in range(halves)]
     returned = []
@@ -713,6 +723,43 @@
         invert_half(2, half)
 
 
+def expand_kernel(z_hbm, index_hbm, motion_hbm, velocity_hbm, out_hbm, z_ref, index_ref, velocity_ref, sem, out_sem):
+    halves, part = z_ref.shape[0], z_ref.shape[3]
+    moves = [
+        pltpu.make_async_copy(z_hbm, z_ref, sem.at[0]),
+        pltpu.make_async_copy(index_hbm, index_ref, sem.at[1]),
+        pltpu.make_async_copy(motion_hbm, out_hbm, sem.at[2]),
+    ]
+    for move in moves:
+        move.start()
+    moves[0].wait()
+    moves[1].wait()
+    length = EPOCHS // PIECES
+    outs = []
+    for piece in range(PIECES):
+
+        def expand(i, carry):
+            e = piece * length + i
+            segment = index_ref[0, e]
+            for half in range(halves):
+                plane = z_ref[half, segment]
+                for component in range(2):
+                    velocity_ref[component, e, pl.ds(half, part, stride=halves), :] = plane[component]
+            return carry
+
+        lax.fori_loop(0, length, expand, 0, unroll=8)
+        for component in range(2):
+            here = (component, pl.ds(piece * length, length))
+            out = pltpu.make_async_copy(
+                velocity_ref.at[here], velocity_hbm.at[here], out_sem.at[component, piece]
+            )
+            out.start()
+            outs.append(out)
+    for out in outs:
+        out.wait()
+    moves[2].wait()
+
+
 def fused(first_image, second_image, prior, offsets, pair_epochs, pair_slot):
     rows, columns = first_image.shape
     steps, halves = rows // SUB, columns // LANES
@@ -722,14 +769,15 @@
     plane = (2, part, LANES)
     split = (2, halves, rows, LANES)
     dma = pltpu.SemaphoreType.DMA
-    return pl.pallas_call(
+    z, index, motion = pl.pallas_call(
         fused_kernel,
         out_shape=(
-            jax.ShapeDtypeStruct((2, EPOCHS, part * halves, LANES), f32),
+            jax.ShapeDtypeStruct((halves, 2 * pairs + 1) + plane, f32),
+            jax.ShapeDtypeStruct((SUB, EPOCHS), i32),
             jax.ShapeDtypeStruct((2, rows, columns), f32),
         ),
-        in_specs=[pl.BlockSpec(memory_space=pltpu.HBM)] * 6,
-        out_specs=(vmem_spec(), vmem_spec()),
+        in_specs=[hbm_spec()] * 6,
+        out_specs=(vmem_spec(),) * 3,
         scratch_shapes=match_scratch(steps, columns)
         + weight_scratch(steps, columns)
         + [
@@ -738,10 +786,8 @@
             pltpu.VMEM(split, f32),
             pltpu.VMEM((ROUNDS, halves, pairs) + plane, f32),
             pltpu.VMEM((halves, pairs) + plane, f32),
-            pltpu.VMEM((halves, 2 * pairs + 1) + plane, f32),
             pltpu.VMEM((halves, pairs) + plane, f32),
             pltpu.VMEM((2 * pairs, LANES), f32),
-            pltpu.VMEM((SUB, EPOCHS), i32),
             pltpu.SMEM((2 * pairs, LANES), f32),
             pltpu.SMEM((SUB, EPOCHS), i32),
             pltpu.SMEM((2, count), i32),
@@ -756,6 +802,25 @@
         compiler_params=params(collective_id=0, has_side_effects=True),
         name="track",
     )(offsets.T, pair_epochs.T, pair_slot, first_image, second_image, prior)
+    whole = (2, EPOCHS, part * halves, LANES)
+    return pl.pallas_call(
+        expand_kernel,
+        out_shape=(
+            jax.ShapeDtypeStruct(whole, f32),
+            jax.ShapeDtypeStruct((2, rows, columns), f32),
+        ),
+        in_specs=[hbm_spec()] * 3,
+        out_specs=(hbm_spec(),) * 2,
+        scratch_shapes=[
+            pltpu.VMEM(z.shape, f32),
+            pltpu.SMEM(index.shape, i32),
+            pltpu.VMEM(whole, f32),
+            dma((3,)),
+            dma((2, PIECES)),
+        ],
+        compiler_params=params(),
+        name="expand",
+    )(z, index, motion)
 
 
 def with_halo(cells, axis, dim, width):

time: 38.4 us -> 37.8 us (0.984)
  local copies, waits for them, and re-layouts: 6.56 us -> 0 us
  Pallas kernels: 30.9 us -> 37 us
    unnamed x14 -> x0, local copies, waits for them, and re-layouts: 6.56 us -> none
    pallas_call x1 -> x2, Pallas kernels: 30.9 us -> 37 us  [the longest x1 31.8 us: fused(): pl.pallas_call(fused_kernel, out_shape=(jax.ShapeDtypeStruct((halves, 2 *...]
where the time goes in v2:
time: 37.8 us; the launch traced here: 37.6 us
  Pallas kernels  37 us (98%)
  between operations  0.64 us (2%)
    pallas_call x1, Pallas kernels, fused(): pl.pallas_call(fused_kernel, out_shape=(jax.ShapeDtypeStruct((halves, 2 *...  31.8 us
    pallas_call x1, Pallas kernels, fused(): pl.pallas_call(expand_kernel, out_shape=(jax.ShapeDtypeStruct(whole, f32)...  5.17 us

profile of v2, /device:TPU:0, one launch (start us, length us, event | category | flops | bytes accessed | tf_op | source)
XLA Modules:
  0.0 37.6 jit_solution(11415725388761076134)
XLA Ops:
  0.6 31.8 %track.1 = (f32[2,17,2,8,128]{4,3,2,1,0:T(8,128)}, s32[8,128]{1,0:T(8,128)}, f32[2,64,256]{2,1,0:T(8,128)}) custom-call(s32[2,64]{1,0:T(2,128)} %bitcast.12, s32[2,8]{1,0:T(2,128)} %bitcast.13, s32[8]{0:T(128)} %slot_hbm.1, f32[64,256]{1,0:T(8,128)} %bitcast.10, f32[64,256]{1,0:T(8,128)} %bitcast.11, f32[2,64,256]{2,1,0:T(8,128)} %bitcast.9), custom_call_target="tpu_custom_call" | custom-call | tf_op jit(solution)/shard_map/track/pallas_call | solution.py:772
  32.4 5.2 %expand.1 = (f32[2,128,16,128]{3,2,1,0:T(8,128)}, f32[2,64,256]{2,1,0:T(8,128)}) custom-call(f32[2,17,2,8,128]{4,3,2,1,0:T(8,128)} %get-tuple-element.7.z_hbm, s32[8,128]{1,0:T(8,128)} %get-tuple-element.8.index_hbm, f32[2,64,256]{2,1,0:T(8,128)} %get-tuple-element.9.motion_hbm), custom_call_target="tpu_custom_call" | custom-call | tf_op jit(solution)/shard_map/expand/pallas_call | solution.py:806

commit v3 on v2

--- a/solution.py
+++ b/solution.py
@@ -27,7 +27,7 @@
 LANES = 128
 AREA = 1.0 / float(WINDOW * WINDOW)
 VMEM_BYTES = 64 * 1024 * 1024
-BLOCK = 4
+BLOCK = 8
 PIECES = 4
 
 
@@ -516,7 +516,7 @@
     first_hbm,
     second_hbm,
     prior_hbm,
-    z_ref,
+    out_ref,
     index_vmem,
     motion_ref,
     image_ref,
@@ -534,6 +534,7 @@
     back_ref,
     d_ref,
     gz_ref,
+    z_ref,
     g_ref,
     coef_vmem,
     coef_ref,
@@ -687,6 +688,11 @@
             for p in range(pairs):
                 gz_ref[half, p] = sums[p]
             return
+        for segment in range(2 * pairs + 1):
+            for component in range(2):
+                out_ref[segment, component, pl.ds(half, part, stride=halves), :] = z_ref[
+                    half, segment, component
+                ]
 
     sent = [match_half(0, half) for half in range(halves)]
     returned = []
@@ -724,7 +730,6 @@
 
 
 def expand_kernel(z_hbm, index_hbm, motion_hbm, velocity_hbm, out_hbm, z_ref, index_ref, velocity_ref, sem, out_sem):
-    halves, part = z_ref.shape[0], z_ref.shape[3]
     moves = [
         pltpu.make_async_copy(z_hbm, z_ref, sem.at[0]),
         pltpu.make_async_copy(index_hbm, index_ref, sem.at[1]),
@@ -740,11 +745,7 @@
 
         def expand(i, carry):
             e = piece * length + i
-            segment = index_ref[0, e]
-            for half in range(halves):
-                plane = z_ref[half, segment]
-                for component in range(2):
-                    velocity_ref[component, e, pl.ds(half, part, stride=halves), :] = plane[component]
+            velocity_ref[:, e] = z_ref[index_ref[0, e]]
             return carry
 
         lax.fori_loop(0, length, expand, 0, unroll=8)
@@ -772,7 +773,7 @@
     z, index, motion = pl.pallas_call(
         fused_kernel,
         out_shape=(
-            jax.ShapeDtypeStruct((halves, 2 * pairs + 1) + plane, f32),
+            jax.ShapeDtypeStruct((2 * pairs + 1, 2, part * halves, LANES), f32),
             jax.ShapeDtypeStruct((SUB, EPOCHS), i32),
             jax.ShapeDtypeStruct((2, rows, columns), f32),
         ),
@@ -786,6 +787,7 @@
             pltpu.VMEM(split, f32),
             pltpu.VMEM((ROUNDS, halves, pairs) + plane, f32),
             pltpu.VMEM((halves, pairs) + plane, f32),
+            pltpu.VMEM((halves, 2 * pairs + 1) + plane, f32),
             pltpu.VMEM((halves, pairs) + plane, f32),
             pltpu.VMEM((2 * pairs, LANES), f32),
             pltpu.SMEM((2 * pairs, LANES), f32),

time: 37.8 us -> 36.3 us (0.960)
  Pallas kernels: 37 us -> 35.5 us
    pallas_call x1, Pallas kernels: 31.8 us -> 30.3 us  [fused(): pl.pallas_call(fused_kernel, out_shape=(jax.ShapeDtypeStruct((2 * pairs +...]
where the time goes in v3:
time: 36.3 us; the launch traced here: 36.1 us
  Pallas kernels  35.5 us (98%)
  between operations  0.64 us (2%)
    pallas_call x1, Pallas kernels, fused(): pl.pallas_call(fused_kernel, out_shape=(jax.ShapeDtypeStruct((2 * pairs +...  30.3 us
    pallas_call x1, Pallas kernels, fused(): pl.pallas_call(expand_kernel, out_shape=(jax.ShapeDtypeStruct(whole, f32)...  5.17 us

profile of v3, /device:TPU:0, one launch (start us, length us, event | category | flops | bytes accessed | tf_op | source)
XLA Modules:
  0.0 36.1 jit_solution(16062174414001309063)
XLA Ops:
  0.6 30.3 %track.1 = (f32[17,2,16,128]{3,2,1,0:T(8,128)}, s32[8,128]{1,0:T(8,128)}, f32[2,64,256]{2,1,0:T(8,128)}) custom-call(s32[2,64]{1,0:T(2,128)} %bitcast.12, s32[2,8]{1,0:T(2,128)} %bitcast.13, s32[8]{0:T(128)} %slot_hbm.1, f32[64,256]{1,0:T(8,128)} %bitcast.10, f32[64,256]{1,0:T(8,128)} %bitcast.11, f32[2,64,256]{2,1,0:T(8,128)} %bitcast.9), custom_call_target="tpu_custom_call" | custom-call | tf_op jit(solution)/shard_map/track/pallas_call | solution.py:773
  31.0 5.2 %expand.1 = (f32[2,128,16,128]{3,2,1,0:T(8,128)}, f32[2,64,256]{2,1,0:T(8,128)}) custom-call(f32[17,2,16,128]{3,2,1,0:T(8,128)} %get-tuple-element.7.z_hbm, s32[8,128]{1,0:T(8,128)} %get-tuple-element.8.index_hbm, f32[2,64,256]{2,1,0:T(8,128)} %get-tuple-element.9.motion_hbm), custom_call_target="tpu_custom_call" | custom-call | tf_op jit(solution)/shard_map/expand/pallas_call | solution.py:808
